TPU v7x, 256 devices: a whole 4x4x8 slice. The times are simulated.
256 devices in a mesh: band: 8 (over x, core), tile: 32 (over y, z).
Axes of the slice: x: 4, y: 4, z: 8, core: 2. Of those that a mesh axis runs over, the one named last changes fastest.
Arguments:
- wind_read: bfloat16 [8, 128, 8192], P(None, 'band', 'tile'), may hold values from -4 to 4
- temp_read: bfloat16 [8, 128, 8192], P(None, 'band', 'tile'), may hold values from 0.69921875 to 1.296875
- diff_read: bfloat16 [8, 128, 8192], P(None, 'band', 'tile'), may hold values from 0.1 to 8400
- removal_read: bfloat16 [8, 128, 8192], P(None, 'band', 'tile'), may hold values from 0.049804688 to 0.5
- frac: float32 [40960, 128], P(('band', 'tile')), may hold values from 0 to 1
- height: float32 [40960, 128], P(('band', 'tile')), may hold values from 0 to 127
- mass: float32 [40960, 128], P(('band', 'tile')), may hold values from 0.5 to 2
- noise: float32 [40960, 128], P(('band', 'tile')), may hold values from -5 to 5
- column: int32 [40960, 128], P(('band', 'tile')), may hold values from 0 to 255
- dest: int32 [40960], P(('band', 'tile')), may hold values from 0 to 31, as said below
Outputs:
- concentration: float32 [8, 128, 8192], P('band', None, 'tile')
- moved_height: float32 [81920, 128], P(('band', 'tile'))
Inputs may be any that keep to these rules, and one draw needn't show every extreme that they name: `dest`: among the 160 blocks of one device no tile is named by more than 10; in every band one tile is named by exactly 10 blocks of every device of the band.
All inputs are finite; a program needn't handle non-finite values.
Results may differ from a plain program's by a relative error of at most 0.0045.
Values may be sent and summed in bfloat16 or wider, within the bound.
A program may use at most 64 MiB of HBM per device.

v0:
```python
import math

import jax
import jax.numpy as jnp
from jax import lax
from jax.sharding import PartitionSpec as P


def passed_along(value, axis, steps):
    count = lax.axis_size(axis)
    pairs = [(source, (source + steps) % count) for source in range(count)]
    return lax.ppermute(value, axis, pairs)


def implicit_diffusion(binned, kdiff):
    kappa = 0.5 * (kdiff[:-1] + kdiff[1:])
    zero_row = jnp.zeros_like(kdiff[:1])
    upper = jnp.concatenate([kappa, zero_row], axis=0)
    lower = jnp.concatenate([zero_row, kappa], axis=0)
    diag = 1.0 + upper + lower

    def forward(carry, inputs):
        prev_c, prev_d = carry
        sub, mid, sup, rhs = inputs
        pivot = mid - sub * prev_c
        new_c = sup / pivot
        new_d = (rhs - sub * prev_d) / pivot
        return ((new_c, new_d), (new_c, new_d))

    start = jnp.zeros_like(binned[0])
    _, (coef_c, coef_d) = lax.scan(forward, (start, start), (-lower, diag, -upper, binned))

    def backward(carry, inputs):
        cval, dval = inputs
        value = dval - cval * carry
        return (value, value)

    _, solved = lax.scan(backward, start, (coef_c, coef_d), reverse=True)
    return solved


def shards(wind_read, temp_read, diff_read, removal_read, frac, height, mass, noise, column, dest):
    stacked = jnp.stack([wind_read, temp_read, diff_read, removal_read])
    owned = lax.all_to_all(stacked, "band", split_axis=1, concat_axis=2, tiled=True)
    levels = owned.shape[2]
    cols = owned.shape[3]
    table = owned.reshape(4 * levels, cols)
    east = passed_along(table[:, 0], "tile", -1)
    east_f = east.astype(jnp.float32)
    kdiff = owned[2, 0].astype(jnp.float32)
    ntile = lax.axis_size("tile")
    nblocks = frac.shape[0]
    width = frac.shape[1]
    cap = 2 * nblocks // ntile
    records = jnp.stack([frac, height, mass, noise, column.astype(jnp.float32)], axis=1)
    onehot = (dest[:, None] == jnp.arange(ntile, dtype=jnp.int32)[None, :]).astype(jnp.int32)
    before = jnp.cumsum(onehot, axis=0) - onehot
    rank = jnp.sum(before * onehot, axis=1)
    slot = dest * cap + rank
    sending = jnp.zeros((ntile * cap, 5, width), jnp.float32).at[slot].set(records)
    sending = sending.reshape(ntile, cap, 5, width)
    level_col = jnp.arange(levels, dtype=jnp.float32)[:, None]
    level_row = jnp.arange(levels, dtype=jnp.float32)[None, :]
    col_ids = jnp.arange(cols, dtype=jnp.int32)[:, None]
    col_row = jnp.arange(cols, dtype=jnp.int32)[None, :]
    zero_bf = jnp.zeros((), jnp.bfloat16)

    def particle_group(fields, start, group):
        part = lax.dynamic_slice_in_dim(fields, start, group, 1)
        frac_r = part[0]
        height_r = part[1]
        mass_r = part[2]
        noise_r = part[3]
        col = part[4].astype(jnp.int32)
        right = frac_r.astype(jnp.bfloat16)
        left = (1.0 - frac_r).astype(jnp.bfloat16)
        weights = jnp.where(col_ids == col[None, :], left[None, :], zero_bf)
        weights = weights + jnp.where(col_ids == col[None, :] + 1, right[None, :], zero_bf)
        edge = jnp.where(col == cols - 1, right.astype(jnp.float32), 0.0)
        horiz = (
            jnp.dot(table, weights, preferred_element_type=jnp.float32)
            + east_f[:, None] * edge[None, :]
        )
        horiz = horiz.reshape(4, levels, group)
        tent = jnp.maximum(0.0, 1.0 - jnp.abs(height_r[None, :] - level_col))
        value = jnp.sum(horiz * tent[None], axis=1)
        znew = jnp.clip(height_r + value[0] + jnp.sqrt(2.0 * value[2]) * noise_r, 0.0, levels - 1.0)
        moved = jnp.where(mass_r > 0, znew, 0.0)
        load = mass_r * jnp.exp(-value[3]) * value[1]
        tent_new = jnp.maximum(0.0, 1.0 - jnp.abs(znew[:, None] - level_row))
        loads = (load[:, None] * tent_new).astype(jnp.bfloat16)
        return (moved, loads)

    received = lax.all_to_all(sending, "tile", split_axis=0, concat_axis=0, tiled=True)
    lead = received.shape[:2]
    count = lead[0] * lead[1]
    total = count * width
    fields = jnp.moveaxis(received.reshape(count, 5, width), 1, 0).reshape(5, total)
    group = math.gcd(total, 2048)
    steps = total // group

    def one_step(carry, index):
        moved, loads = particle_group(fields, index * group, group)
        return (carry, (moved, loads))

    _, (moved, loads) = lax.scan(one_step, 0, jnp.arange(steps, dtype=jnp.int32))
    cols_out = fields[4].astype(jnp.int32)
    moved, loads, cols_out = (
        moved.reshape(lead + (width,)),
        loads.reshape(lead + (width, levels)),
        cols_out.reshape(lead + (width,)),
    )
    total_slots = ntile * cap
    total_rows = total_slots * width
    bin_rows = math.gcd(total_rows, 2048)
    load_groups = loads.reshape(total_rows // bin_rows, bin_rows, levels)
    col_groups = cols_out.reshape(total_rows // bin_rows, bin_rows)

    def add_group(total, item):
        load_part, col_part = item
        selector = (col_part[:, None] == col_row).astype(jnp.bfloat16)
        product = lax.dot_general(
            load_part, selector, (((0,), (0,)), ((), ())), preferred_element_type=jnp.float32
        )
        return (total + product, None)

    binned, _ = lax.scan(
        add_group, jnp.zeros((levels, cols), jnp.float32), (load_groups, col_groups)
    )
    conc = implicit_diffusion(binned, kdiff)
    return (conc[None], moved.reshape(total_slots, width))


def solution(mesh):
    in_specs = (
        P(None, "band", "tile"),
        P(None, "band", "tile"),
        P(None, "band", "tile"),
        P(None, "band", "tile"),
        P(("band", "tile"), None),
        P(("band", "tile"), None),
        P(("band", "tile"), None),
        P(("band", "tile"), None),
        P(("band", "tile"), None),
        P(("band", "tile")),
    )
    out_specs = (P("band", None, "tile"), P(("band", "tile"), None))
    return jax.shard_map(shards, mesh=mesh, in_specs=in_specs, out_specs=out_specs, check_vma=False)
```

profile of v0, /device:TPU:1, one launch (start us, length us, event | category | flops | bytes accessed | tf_op | source)
XLA Modules:
  0.0 232.3 jit_solution(10074575185461880837)
XLA Ops:
  0.6 1.7 pad_maximum_fusion
  2.3 6.6 %all-to-all-start = ((bf16[4,8,16,256]{3,2,0,1:T(8,128)(2,1)}), bf16[4,8,16,256]{3,2,0,1:T(8,128)(2,1)S(1)}, u32[]{:S(2)}, u32[]{:S(2)}) async-start(bf16[4,8,16,256]{3,2,0,1:T(8,128)(2,1)} %pad_maximum_fusion), calls=%async_computation | async-start | bytes 524288 | tf_op jit(solution)/shard_map/all_to_all | solution.py:44
  15.3 5.2 %scatter_fusion = f32[320,5,128]{2,1,0:T(8,128)S(1)} fusion(f32[320,5,128]{2,1,0:T(8,128)S(1)} %broadcast_in_dim.83, s32[160]{0:T(256)S(1)} %compare_select_fusion.2, f32[160,5,128]{2,1,0:T(8,128)S(1)} %copy.24), kind=kCustom, calls=%fused_computation | custom fusion | bytes 1229440 | tf_op jit(solution)/shard_map/scatter | solution.py:60
  21.9 10.5 %all-to-all-start.1 = ((f32[32,10,5,128]{3,1,2,0:T(8,128)}), f32[32,10,5,128]{3,1,2,0:T(8,128)S(1)}, u32[]{:S(2)}, u32[]{:S(2)}) async-start(f32[32,10,5,128]{3,1,2,0:T(8,128)} %copy.26), calls=%async_computation.1 | async-start | bytes 2621440 | tf_op jit(solution)/shard_map/all_to_all | solution.py:94
  32.5 4.7 %collective-permute-start = (bf16[512]{0:T(512)(128)(2,1)S(1)}, bf16[512]{0:T(512)(128)(2,1)S(1)}, u32[]{:S(2)}, u32[]{:S(2)}) collective-permute-start(bf16[512]{0:T(512)(128)(2,1)S(1)} %slice_reduce_fusion), channel_id=1, source_target_pairs={{0,31},{1,0},{2,1},{3,2},{4,3},{5,4},{6,5},{7,6},{8,7},{9,8},{10,9... | collective-permute-start | bytes 3080 | tf_op jit(solution)/shard_map/ppermute | solution.py:12
  37.3 25.0 %collective-permute-done = bf16[512]{0:T(512)(128)(2,1)S(1)} collective-permute-done((bf16[512]{0:T(512)(128)(2,1)S(1)}, bf16[512]{0:T(512)(128)(2,1)S(1)}, u32[]{:S(2)}, u32[]{:S(2)}) %collective-permute-start) | collective-permute-done | bytes 1056 | tf_op jit(solution)/shard_map/ppermute | solution.py:12
  62.4 1.7 all-to-all-done.1
  64.9 95.1 %while.59 = (s32[]{:T(128)}, f32[20,2048]{1,0:T(8,128)S(1)}, bf16[20,2048,128]{2,1,0:T(8,128)(2,1)}, s32[20]{0:T(128)S(1)}, f32[5,40960]{1,0:T(8,128)S(1)}, /*in...) while((s32[]{:T(128)}, f32[20,2048]{1,0:T(8,128)S(1)}, ...), condition=%wide.region_6.7_spmd.clone.clone, body=%wide.region_4.6_spmd.clone.clone.sunk | while | flops 547915776 | bytes 3193627 | solution.py:106
  72.7 1.4 fusion.55
  77.5 1.4 fusion.55
  82.3 1.4 fusion.55
  87.0 1.4 fusion.55
  91.8 1.4 fusion.55
  101.3 1.4 fusion.55
  106.0 1.4 fusion.55
  110.7 1.4 fusion.55
  115.5 1.4 fusion.55
  120.3 1.4 fusion.55
  125.0 1.4 fusion.55
  129.8 1.4 fusion.55
  139.3 1.4 fusion.55
  144.0 1.5 fusion.55
  148.8 1.5 fusion.55
  153.6 1.4 fusion.55
  158.4 1.4 fusion.55
  160.0 35.9 %while.60 = (s32[]{:T(128)}, f32[128,256]{1,0:T(8,128)S(1)}, bf16[20,2048,128]{2,1,0:T(8,128)(2,1)}, s32[20,2048]{1,0:T(8,128)S(1)}, s32[]{:T(128)}, /*index=5*/s32[]{:T(128)}) while((s32[]{:T(128)}, f32[128,256]{1,0:T(8,128)S(1)}, bf16[20,2048,128]{2,1,0:T(8,128)(2,1)}, s32[20,2048]{1,0:T(8,128)S(1)}, s32[]{:T(128)}, ...), condition=%wide.region_8.9_spmd.clone, body=%wide.region_7.8_spmd.clone.sunk | while | flops 134807552 | bytes 811603 | solution.py:127
  160.1 1.7 fusion.57
  161.9 1.7 fusion.57
  163.7 1.7 fusion.57
  165.4 1.7 fusion.57
  167.2 1.7 fusion.57
  169.0 1.7 fusion.57
  170.8 1.7 fusion.57
  172.6 1.7 fusion.57
  174.4 1.7 fusion.57
  176.2 1.7 fusion.57
  178.0 1.7 fusion.57
  179.8 1.7 fusion.57
  181.6 1.7 fusion.57
  183.4 1.7 fusion.57
  185.2 1.7 fusion.57
  187.0 1.7 fusion.57
  188.8 1.7 fusion.57
  190.6 1.7 fusion.57
  192.4 1.7 fusion.57
  194.1 1.7 fusion.57
  195.9 22.3 %while.61 = (s32[]{:T(128)}, f32[256]{0:T(256)S(1)}, f32[256]{0:T(256)S(1)}, f32[128,256]{1,0:T(8,128)S(1)}, f32[128,256]{1,0:T(8,128)S(1)}, /*index=5*/f32[128,...) while((s32[]{:T(128)}, f32[256]{0:T(256)S(1)}, ...), condition=%wide.region_10.11_spmd.clone, body=%wide.region_9.10_spmd.clone.sunk | while | flops 2051 | bytes 20615 | solution.py:31
  218.3 13.3 %while.62 = (s32[]{:T(128)}, f32[256]{0:T(256)S(1)}, f32[128,256]{1,0:T(8,128)S(1)}, f32[128,256]{1,0:T(8,128)S(1)}, f32[128,256]{1,0:T(8,128)S(1)}, /*index=5*/s32[]{:T(128)}, s32[]{:T(128)}, s32[]{:T(128)}) while((s32[]{:T(128)}, f32[256]{0:T(256)S(1)}, f32[128,256]{1,0:T(8,128)S(1)}, f32[128,256]{1,0:T(8,128)S(1)}, ...), condition=%wide.region_12.13_spmd.clone, body=%wide.region_11.12_spmd.clone.sunk | while | flops 772 | bytes 10355 | solution.py:38
  (1274 shorter events, 90.7 us)
Async XLA Ops:
  0.6 14.3 %copy-start.1 = (s32[160]{0:T(256)S(1)}, s32[160]{0:T(256)}, u32[]{:S(2)}) copy-start(s32[160]{0:T(256)} %param.27) | copy-start | bytes 1924
  2.3 19.6 %all-to-all-start = ((bf16[4,8,16,256]{3,2,0,1:T(8,128)(2,1)}), bf16[4,8,16,256]{3,2,0,1:T(8,128)(2,1)S(1)}, u32[]{:S(2)}, u32[]{:S(2)}) async-start(bf16[4,8,16,256]{3,2,0,1:T(8,128)(2,1)} %pad_maximum_fusion), calls=%async_computation | async-start | bytes 524288 | tf_op jit(solution)/shard_map/all_to_all | solution.py:44
  21.9 42.2 %all-to-all-start.1 = ((f32[32,10,5,128]{3,1,2,0:T(8,128)}), f32[32,10,5,128]{3,1,2,0:T(8,128)S(1)}, u32[]{:S(2)}, u32[]{:S(2)}) async-start(f32[32,10,5,128]{3,1,2,0:T(8,128)} %copy.26), calls=%async_computation.1 | async-start | bytes 2621440 | tf_op jit(solution)/shard_map/all_to_all | solution.py:94
  32.5 29.8 %collective-permute-start = (bf16[512]{0:T(512)(128)(2,1)S(1)}, bf16[512]{0:T(512)(128)(2,1)S(1)}, u32[]{:S(2)}, u32[]{:S(2)}) collective-permute-start(bf16[512]{0:T(512)(128)(2,1)S(1)} %slice_reduce_fusion), channel_id=1, source_target_pairs={{0,31},{1,0},{2,1},{3,2},{4,3},{5,4},{6,5},{7,6},{8,7},{9,8},{10,9... | collective-permute-start | bytes 3080 | tf_op jit(solution)/shard_map/ppermute | solution.py:12
  64.8 95.2 %copy-start.2 = (f32[128,256]{1,0:T(8,128)S(1)}, f32[128,256]{1,0:T(8,128)}, u32[]{:S(2)}) copy-start(f32[128,256]{1,0:T(8,128)} %custom-call) | copy-start | bytes 393220
  231.6 0.7 copy-start
where the time goes:
time: 236 us; the launch traced here: 232 us
  matrix products  60.2 us (26%)
  local copies, waits for them, and re-layouts  49.7 us (21%)
  other arithmetic  46.9 us (20%)
  waiting for transfers between devices  26.8 us (11%)
  loops' own time  26.1 us (11%)
  starting transfers between devices  21.7 us (9%)
    dot_general x20, matrix products, add_group(): lax.dot_general(load_part, selector, (((0,), (0,)), ((), ())), preferred_...  34.9 us
    dynamic_update_slice x20, other arithmetic, shards(): lax.scan(one_step, 0, jnp.arange(steps, dtype=jnp.int32))  28.5 us
    dot_general x20, matrix products, particle_group(): jnp.dot(table, weights, preferred_element_type=jnp.float32)  25.2 us
    ppermute x1, waiting for transfers between devices, passed_along(): return lax.ppermute(value, axis, pairs)  25 us
    dynamic_update_slice x384, local copies, waits for them, and re-layouts, implicit_diffusion(): lax.scan(forward, (start, start), (-lower, diag, -upper, binned))  16.6 us
    another operation x1, loops' own time, shards(): lax.scan(one_step, 0, jnp.arange(steps, dtype=jnp.int32))  14.7 us
    dynamic_slice x20, local copies, waits for them, and re-layouts, shards(): lax.scan(one_step, 0, jnp.arange(steps, dtype=jnp.int32))  12.9 us
    all_to_all x1, starting transfers between devices, shards(): lax.all_to_all(sending, 'tile', split_axis=0, concat_axis=0, tiled=True)  10.5 us
  transfers between devices with their start and end apart: 3, of which 2 were waited for; matrix products, arithmetic and copies ran while one was open for 6% of the time, Pallas kernels for 0%

commit v1 on v0

v1 whole, which is shorter than its diff:
```python
import jax
import jax.numpy as jnp
from jax import lax
from jax.experimental import pallas as pl
from jax.experimental.pallas import tpu as pltpu
from jax.sharding import PartitionSpec as P

LEV = 128
COLS = 256
CAP = 10
PB = 128
CH = 2
F32 = jnp.float32
BF = jnp.bfloat16


def iota(shape, dim, dtype=F32):
    return lax.broadcasted_iota(jnp.int32, shape, dim).astype(dtype)


def split_levels(table_ref, tperm_ref):
    row = lax.broadcasted_iota(jnp.int32, (LEV, LEV), 0)
    col = lax.broadcasted_iota(jnp.int32, (LEV, LEV), 1)
    source = jnp.where(row < LEV // 2, 2 * row, 2 * row - (LEV - 1))
    perm = (col == source).astype(F32).astype(BF)
    for f in range(4):
        part = pl.ds(f * LEV, LEV)
        tperm_ref[part, :] = jnp.dot(perm, table_ref[part, :], preferred_element_type=F32).astype(BF)


def set_kappa(table_ref, upper_ref, lower_ref):
    k = table_ref[pl.ds(2 * LEV, LEV), :].astype(F32)
    kappa = 0.5 * (k[:-1] + k[1:])
    zero = jnp.zeros((1, COLS), F32)
    upper_ref[...] = jnp.concatenate([kappa, zero], axis=0)
    lower_ref[...] = jnp.concatenate([zero, kappa], axis=0)


def pivots(step, carry, upper_ref, lower_ref, inv_ref):
    top, bot = carry
    for i in range(2):
        k = 2 * step + i
        u = upper_ref[pl.ds(k, 1), :]
        inv = 1.0 / (top + u)
        inv_ref[pl.ds(k, 1), :] = inv
        last_top = top
        top = 1.0 + u * (top * inv)
        m = LEV - 1 - k
        low = lower_ref[pl.ds(m, 1), :]
        inv = 1.0 / (bot + low)
        inv_ref[pl.ds(m, 1), :] = inv
        last_bot = bot
        bot = 1.0 + low * (bot * inv)
    return (top, bot), (last_top, last_bot)


def interpolate(fr, height, col, tperm_ref, val_ref):
    left = (1.0 - fr)
    low = jnp.clip(jnp.floor(height), 0.0, LEV - 2.0)
    odd_i = jnp.floor(low * 0.5)
    even_i = jnp.floor((low + 1.0) * 0.5)
    w_even = jnp.maximum(0.0, 1.0 - jnp.abs(height - 2.0 * even_i))
    w_odd = jnp.maximum(0.0, 1.0 - jnp.abs(height - (2.0 * odd_i + 1.0)))
    g_even = jnp.floor(even_i * 0.125)
    g_odd = jnp.floor(odd_i * 0.125)
    s_even = even_i - 8.0 * g_even
    s_odd = odd_i - 8.0 * g_odd
    ids = iota((COLS, PB), 0, BF)
    sub = iota((8, PB), 0)
    zero = jnp.zeros((COLS, PB), BF)

    def spread(x, c, rows, dtype=F32):
        return jnp.broadcast_to(x[c:c + 1], (rows, PB)).astype(dtype)

    for c0 in range(0, CAP, CH):
        weights = []
        for c in range(c0, c0 + CH):
            cb = spread(col, c, COLS, BF)
            cb1 = spread(col + 1.0, c, COLS, BF)
            lb = spread(left, c, COLS, BF)
            rb = spread(fr, c, COLS, BF)
            weights.append(jnp.where(ids == cb, lb, jnp.where(ids == cb1, rb, zero)))
        horiz = jnp.dot(tperm_ref[...], jnp.concatenate(weights, axis=1), preferred_element_type=F32)
        for i in range(CH):
            c = c0 + i
            ge = spread(g_even, c, 8)
            go = spread(g_odd, c, 8)
            we = jnp.where(sub == spread(s_even, c, 8), spread(w_even, c, 8), 0.0)
            wo = jnp.where(sub == spread(s_odd, c, 8), spread(w_odd, c, 8), 0.0)
            e_masks = [ge >= float(g) for g in range(1, 8)]
            o_masks = [go >= float(g) for g in range(1, 8)]
            lanes = slice(i * PB, (i + 1) * PB)
            for f in range(4):
                base = f * LEV
                e = horiz[base:base + 8, lanes]
                o = horiz[base + 64:base + 72, lanes]
                for g in range(1, 8):
                    e = jnp.where(e_masks[g - 1], horiz[base + 8 * g:base + 8 * g + 8, lanes], e)
                    o = jnp.where(o_masks[g - 1], horiz[base + 64 + 8 * g:base + 72 + 8 * g, lanes], o)
                val_ref[f, c:c + 1, :] = jnp.sum(e * we + o * wo, axis=0, keepdims=True)


def move(fr, height, noise, mass, col, val, east):
    low = jnp.clip(jnp.floor(height), 0.0, LEV - 2.0)
    fz = height - low
    right = fr.astype(BF).astype(F32)
    edge = jnp.where(col == COLS - 1.0, right, 0.0)
    low_i = low.astype(jnp.int32)
    pad = jnp.zeros((16 - CAP, PB), jnp.int32)
    low_p = jnp.concatenate([low_i, pad], axis=0)
    out = []
    for f in range(4):
        lo = jnp.concatenate([jnp.take_along_axis(east[f], low_p[r:r + 8], axis=1) for r in (0, 8)], axis=0)[:CAP]
        hi = jnp.concatenate([jnp.take_along_axis(east[f], low_p[r:r + 8] + 1, axis=1) for r in (0, 8)], axis=0)[:CAP]
        out.append(val[f] + edge * (lo * (1.0 - fz) + hi * fz))
    w, temp, kd, rate = out
    znew = jnp.clip(height + w + jnp.sqrt(2.0 * kd) * noise, 0.0, LEV - 1.0)
    moved = jnp.where(mass > 0, znew, 0.0)
    load = mass * jnp.exp(-rate) * temp
    low = jnp.clip(jnp.floor(znew), 0.0, LEV - 2.0)
    fz = znew - low
    return moved, low, load * (1.0 - fz), load * fz


def binning(low, load_lo, load_hi, col):
    lev = iota((LEV, PB), 0, BF)
    ids = iota((COLS, PB), 0, BF)
    one = jnp.ones((COLS, PB), BF)
    loads, picks = [], []
    for c in range(CAP):
        lb = jnp.broadcast_to(low[c:c + 1], (LEV, PB)).astype(BF)
        hb = jnp.broadcast_to(low[c:c + 1] + 1.0, (LEV, PB)).astype(BF)
        a = jnp.broadcast_to(load_lo[c:c + 1], (LEV, PB)).astype(BF)
        b = jnp.broadcast_to(load_hi[c:c + 1], (LEV, PB)).astype(BF)
        loads.append(jnp.where(lev == lb, a, jnp.where(lev == hb, b, jnp.zeros_like(a))))
        cb = jnp.broadcast_to(col[c:c + 1], (COLS, PB)).astype(BF)
        picks.append(jnp.where(ids == cb, one, jnp.zeros_like(one)))
    return lax.dot_general(jnp.concatenate(picks, axis=1), jnp.concatenate(loads, axis=1),
                           (((1,), (1,)), ((), ())), preferred_element_type=F32)


def solve(ends, binned, upper_ref, lower_ref, inv_ref, rhs_ref, fwd_ref, back_ref, out_ref):
    top, bot = ends
    half = LEV // 2
    inv = inv_ref[...]
    u, low = upper_ref[...], lower_ref[...]
    upper_rows = lax.broadcasted_iota(jnp.int32, (LEV, COLS), 0) < half
    rhs_ref[...] = binned * inv
    fwd_ref[...] = jnp.where(upper_rows, low, u) * inv
    back_ref[...] = jnp.where(upper_rows, u, low) * inv
    d = rhs_ref[0:1, :]
    e = rhs_ref[LEV - 1:LEV, :]
    ds, es = [d], [e]
    for k in range(1, half):
        m = LEV - 1 - k
        d = rhs_ref[k:k + 1, :] + fwd_ref[k:k + 1, :] * d
        e = rhs_ref[m:m + 1, :] + fwd_ref[m:m + 1, :] * e
        ds.append(d)
        es.append(e)
    kappa = upper_ref[half - 1:half, :]
    alpha = back_ref[half - 1:half, :]
    beta = back_ref[half:half + 1, :]
    det = (kappa * (top + bot) + top * bot) * inv_ref[half - 1:half, :] * inv_ref[half:half + 1, :]
    x = (d + alpha * e) / det
    y = e + beta * x
    out_ref[half - 1:half, :] = x
    out_ref[half:half + 1, :] = y
    for k in range(half - 2, -1, -1):
        m = LEV - 1 - k
        x = ds[k] + back_ref[k:k + 1, :] * x
        y = es[k] + back_ref[m:m + 1, :] * y
        out_ref[k:k + 1, :] = x
        out_ref[m:m + 1, :] = y


N_BAND = 8
N_TILE = 32
NY, NZ = 4, 8
B_DEV = 160
SUB = LEV // N_BAND
ROWS = 4 * CAP


def offset(i):
    q, dy = i // NY, i % NY
    dz = ((q + 1) // 2) * (q % 2) + ((NZ - q // 2) % NZ) * (1 - q % 2)
    return dy, dz


def place(tile, i, sign):
    dy, dz = offset(i)
    y = (tile // NZ + NY + sign * dy) % NY
    z = (tile % NZ + NZ + sign * dz) % NZ
    return y * NZ + z


def build(dest_ref, parts, col_ref, send_f, send_c):
    dest = dest_ref[...].astype(F32)
    wide = jnp.broadcast_to(dest, (B_DEV, B_DEV))
    row = lax.broadcasted_iota(jnp.int32, (B_DEV, B_DEV), 0)
    lane = lax.broadcasted_iota(jnp.int32, (B_DEV, B_DEV), 1)
    tall = jnp.sum(jnp.where(row == lane, wide, 0.0), axis=1, keepdims=True)
    same = jnp.where((tall == wide) & (row < lane), 1.0, 0.0)
    rank = jnp.sum(same, axis=0, keepdims=True)
    slots = N_TILE * CAP
    pick = jnp.where(iota((slots, B_DEV), 0) == dest * CAP + rank, 1.0, 0.0).astype(BF)
    for f, ref in enumerate(parts):
        x = ref[...]
        hi = x.astype(BF)
        rest = x - hi.astype(F32)
        mid = rest.astype(BF)
        low = (rest - mid.astype(F32)).astype(BF)
        total = jnp.dot(pick, hi, preferred_element_type=F32)
        total = total + jnp.dot(pick, mid, preferred_element_type=F32)
        total = total + jnp.dot(pick, low, preferred_element_type=F32)
        send_f[pl.ds(f, slots, stride=4), :] = total
    pick = jnp.where(iota((N_TILE * 16, B_DEV), 0) == dest * 16 + rank, 1.0, 0.0).astype(BF)
    cols = jnp.dot(pick, col_ref[...].astype(F32).astype(BF), preferred_element_type=F32)
    send_c[...] = cols.astype(BF).reshape(N_TILE, 16, PB)


def kernel(wind, temp, diff, removal, frac, height, noise, mass, column, dest,
           conc_ref, moved_ref,
           table, tperm, east_out, east_in, send_f, send_c, recv_f, recv_c,
           val, binned, upper, lower, inv, rhs, fwd, back,
           field_send, field_recv, own_sem, east_sems, f_send, f_recv, c_send, c_recv):
    band, tile = lax.axis_index("band"), lax.axis_index("tile")
    barrier = pltpu.get_barrier_semaphore()

    def greet_tile(i, _):
        pl.semaphore_signal(barrier, inc=1, device_id=(band, place(tile, i, 1)), device_id_type=pl.DeviceIdType.MESH)
        return 0

    def greet_band(i, _):
        pl.semaphore_signal(barrier, inc=1, device_id=((band + i) % N_BAND, tile), device_id_type=pl.DeviceIdType.MESH)
        return 0

    lax.fori_loop(1, N_TILE, greet_tile, 0)
    lax.fori_loop(1, N_BAND, greet_band, 0)
    fields = (wind, temp, diff, removal)
    own = [pltpu.make_async_copy(ref.at[band], table.at[pl.ds(pl.multiple_of(f * LEV + band * SUB, SUB), SUB)], own_sem.at[f])
           for f, ref in enumerate(fields)]
    for copy in own:
        copy.start()
    build(dest, (frac, height, noise, mass), column, send_f, send_c)
    pl.semaphore_wait(barrier, N_TILE + N_BAND - 2)

    def field_copy(i, f, to, rows_of):
        return pltpu.make_async_remote_copy(
            src_ref=fields[f].at[to], dst_ref=table.at[pl.ds(pl.multiple_of(f * LEV + rows_of * SUB, SUB), SUB)],
            send_sem=field_send.at[i, f], recv_sem=field_recv.at[i, f],
            device_id=(to, tile), device_id_type=pl.DeviceIdType.MESH)

    def record_copies(i, to, slot):
        return [pltpu.make_async_remote_copy(
            src_ref=send_f.at[pl.ds(pl.multiple_of(to * ROWS, 8), ROWS)], dst_ref=recv_f.at[slot],
            send_sem=f_send.at[i], recv_sem=f_recv.at[i],
            device_id=(band, to), device_id_type=pl.DeviceIdType.MESH),
            pltpu.make_async_remote_copy(
            src_ref=send_c.at[to], dst_ref=recv_c.at[slot],
            send_sem=c_send.at[i], recv_sem=c_recv.at[i],
            device_id=(band, to), device_id_type=pl.DeviceIdType.MESH)]

    def send_fields(i, _):
        to = (band + i) % N_BAND
        for f in range(4):
            field_copy(i, f, to, band).start()
        return 0

    def send_records(i, _):
        for copy in record_copies(i, place(tile, i, 1), tile):
            copy.start()
        return 0

    lax.fori_loop(1, N_BAND, send_fields, 0)
    lax.fori_loop(1, N_TILE, send_records, 0)
    recv_f[tile] = send_f[pl.ds(pl.multiple_of(tile * ROWS, 8), ROWS), :]
    recv_c[tile] = send_c[tile]
    binned[...] = jnp.zeros_like(binned)
    for copy in own:
        copy.wait()

    def take_fields(i, _):
        source = (band + N_BAND - i) % N_BAND
        for f in range(4):
            field_copy(i, f, (band + i) % N_BAND, source).wait_recv()
        return 0

    lax.fori_loop(1, N_BAND, take_fields, 0)
    first = jnp.where(lax.broadcasted_iota(jnp.int32, (8, COLS), 1) == 0, 1.0, 0.0).astype(BF)
    east_out[...] = lax.dot_general(first, table[...], (((1,), (1,)), ((), ())), preferred_element_type=F32)
    west = (tile + N_TILE - 1) % N_TILE
    east_copy = pltpu.make_async_remote_copy(
        src_ref=east_out, dst_ref=east_in, send_sem=east_sems.at[0], recv_sem=east_sems.at[1],
        device_id=(band, west), device_id_type=pl.DeviceIdType.MESH)
    east_copy.start()
    split_levels(table, tperm)
    set_kappa(table, upper, lower)
    east_copy.wait()

    def body(i, carry):
        source = place(tile, i, -1)

        @pl.when(i > 0)
        def _():
            for copy in record_copies(i, place(tile, i, 1), source):
                copy.wait_recv()

        carry, ends = pivots(i, carry[0], upper, lower, inv)
        fr = recv_f[source, pl.ds(0, CAP, stride=4), :]
        h = recv_f[source, pl.ds(1, CAP, stride=4), :]
        n = recv_f[source, pl.ds(2, CAP, stride=4), :]
        m = recv_f[source, pl.ds(3, CAP, stride=4), :]
        col = recv_c[source].astype(F32)[:CAP]
        interpolate(fr, h, col, tperm, val)
        east = [east_in[:, f * LEV:(f + 1) * LEV] for f in range(4)]
        moved, low, a, b = move(fr, h, n, m, col, [val[f, 0:CAP, :] for f in range(4)], east)
        moved_ref[source] = moved
        binned[...] += binning(low, a, b, col)
        return carry, ends

    one = jnp.ones((1, COLS), F32)
    _, ends = lax.fori_loop(0, N_TILE, body, ((one, one), (one, one)))
    solve(ends, binned[...].T, upper, lower, inv, rhs, fwd, back, conc_ref)

    def sent_fields(i, _):
        for f in range(4):
            field_copy(i, f, (band + i) % N_BAND, band).wait_send()
        return 0

    def sent_records(i, _):
        for copy in record_copies(i, place(tile, i, 1), tile):
            copy.wait_send()
        return 0

    lax.fori_loop(1, N_BAND, sent_fields, 0)
    lax.fori_loop(1, N_TILE, sent_records, 0)


def shards(wind, temp, diff, removal, frac, height, mass, noise, column, dest):
    vm = pl.BlockSpec(memory_space=pltpu.VMEM)
    hbm = pl.BlockSpec(memory_space=pl.ANY)
    grid = pltpu.VMEM((LEV, COLS), F32)
    dma = pltpu.SemaphoreType.DMA
    conc, moved = pl.pallas_call(
        kernel,
        out_shape=(jax.ShapeDtypeStruct((LEV, COLS), F32), jax.ShapeDtypeStruct((N_TILE, CAP, PB), F32)),
        in_specs=[hbm] * 4 + [vm] * 6,
        out_specs=(vm, vm),
        scratch_shapes=[
            pltpu.VMEM((4 * LEV, COLS), BF), pltpu.VMEM((4 * LEV, COLS), BF),
            pltpu.VMEM((8, 4 * LEV), F32), pltpu.VMEM((8, 4 * LEV), F32),
            pltpu.VMEM((N_TILE * ROWS, PB), F32), pltpu.VMEM((N_TILE, 16, PB), BF),
            pltpu.VMEM((N_TILE, ROWS, PB), F32), pltpu.VMEM((N_TILE, 16, PB), BF),
            pltpu.VMEM((4, 16, PB), F32), pltpu.VMEM((COLS, LEV), F32),
            grid, grid, grid, grid, grid, grid,
            dma((N_BAND, 4)), dma((N_BAND, 4)), dma((4,)), dma((2,)),
            dma((N_TILE,)), dma((N_TILE,)), dma((N_TILE,)), dma((N_TILE,)),
        ],
        compiler_params=pltpu.CompilerParams(
            collective_id=0, has_side_effects=True, vmem_limit_bytes=48 * 2**20),
        cost_estimate=pl.CostEstimate(flops=2 * 40960 * 256 * 640, bytes_accessed=2 * 2**20, transcendentals=0),
    )(wind, temp, diff, removal, frac, height, noise, mass, column, dest.reshape(1, B_DEV))
    return conc[None], moved.reshape(N_TILE * CAP, PB)


def solution(mesh):
    read = P(None, "band", "tile")
    rec = P(("band", "tile"), None)
    return jax.shard_map(
        shards, mesh=mesh,
        in_specs=(read,) * 4 + (rec,) * 5 + (P(("band", "tile")),),
        out_specs=(P("band", None, "tile"), rec), check_vma=False)
```

time: 236 us -> 72.7 us (0.31); the launches traced: 232 us -> 71.9 us
  Pallas kernels: 0 us -> 61.5 us
  matrix products: 60.2 us -> 0 us
  other arithmetic: 46.9 us -> 0 us
  local copies, waits for them, and re-layouts: 49.7 us -> 9.8 us
  waiting for transfers between devices: 26.8 us -> 0 us
  loops' own time: 26.1 us -> 0 us
  starting transfers between devices: 21.7 us -> 0 us
    pallas_call x0 -> x1, Pallas kernels: none -> 61.5 us  [shards(): pl.pallas_call(kernel, out_shape=(jax.ShapeDtypeStruct((LEV, COLS), F32),...]
    dot_general x40 -> x0, matrix products: 60.2 us -> none  [the longest x20 34.9 us: add_group(): lax.dot_general(load_part, selector, (((0,), (0,)), ((), ())), preferred_...]
    dynamic_update_slice x20 -> x0, other arithmetic: 28.5 us -> none  [shards(): lax.scan(one_step, 0, jnp.arange(steps, dtype=jnp.int32))]
    another operation x4 -> x0, loops' own time: 26.1 us -> none  [the longest x1 14.7 us: shards(): lax.scan(one_step, 0, jnp.arange(steps, dtype=jnp.int32))]
    ppermute x1 -> x0, waiting for transfers between devices: 25 us -> none  [passed_along(): return lax.ppermute(value, axis, pairs)]
    dynamic_update_slice x404 -> x0, local copies, waits for them, and re-layouts: 19.7 us -> none  [the longest x384 16.6 us: implicit_diffusion(): lax.scan(forward, (start, start), (-lower, diag, -upper, binned))]
    dynamic_slice x424 -> x0, local copies, waits for them, and re-layouts: 17.7 us -> none  [the longest x20 12.9 us: shards(): lax.scan(one_step, 0, jnp.arange(steps, dtype=jnp.int32))]
    all_to_all x2 -> x0, starting transfers between devices: 17 us -> none  [the longest x1 10.5 us: shards(): lax.all_to_all(sending, 'tile', split_axis=0, concat_axis=0, tiled=True)]
  transfers between devices with their start and end apart: 3 -> 0, of which waited for: 2 -> 0; matrix products, arithmetic and copies ran while one was open for 6% -> 0% of each run, Pallas kernels for 0% -> 0%
where the time goes in v1:
time: 72.7 us; the launch traced here: 71.9 us
  Pallas kernels  61.5 us (85%)
  local copies, waits for them, and re-layouts  9.8 us (13%)
    pallas_call x1, Pallas kernels, shards(): pl.pallas_call(kernel, out_shape=(jax.ShapeDtypeStruct((LEV, COLS), F32),...  61.5 us
    unnamed x21, local copies, waits for them, and re-layouts  9.11 us

profile of v1, /device:TPU:1, one launch (start us, length us, event | category | flops | bytes accessed | tf_op | source)
XLA Modules:
  0.0 71.9 jit_solution(5228944000070259167)
XLA Ops:
  0.6 0.0 copy-start.9
  0.6 0.7 copy-done.9
  1.3 0.0 copy-start
  1.3 0.9 %copy-done = f32[160,128]{1,0:T(8,128)S(1)} copy-done((f32[160,128]{1,0:T(8,128)S(1)}, f32[160,128]{1,0:T(8,128)}, u32[]{:S(2)}) %copy-start) | copy-done | bytes 81944
  2.2 0.0 copy-start.1
  2.2 0.9 %copy-done.1 = f32[160,128]{1,0:T(8,128)S(1)} copy-done((f32[160,128]{1,0:T(8,128)S(1)}, f32[160,128]{1,0:T(8,128)}, u32[]{:S(2)}) %copy-start.1) | copy-done | bytes 81944
  3.1 0.0 copy-start.2
  3.1 0.9 %copy-done.2 = f32[160,128]{1,0:T(8,128)S(1)} copy-done((f32[160,128]{1,0:T(8,128)S(1)}, f32[160,128]{1,0:T(8,128)}, u32[]{:S(2)}) %copy-start.2) | copy-done | bytes 81944
  4.0 0.0 copy-start.3
  4.0 0.9 %copy-done.3 = f32[160,128]{1,0:T(8,128)S(1)} copy-done((f32[160,128]{1,0:T(8,128)S(1)}, f32[160,128]{1,0:T(8,128)}, u32[]{:S(2)}) %copy-start.3) | copy-done | bytes 81944
  4.9 0.0 copy-start.4
  4.9 0.9 %copy-done.4 = s32[160,128]{1,0:T(8,128)S(1)} copy-done((s32[160,128]{1,0:T(8,128)S(1)}, s32[160,128]{1,0:T(8,128)}, u32[]{:S(2)}) %copy-start.4) | copy-done | bytes 81944
  5.8 0.0 copy-start.5
  5.8 0.8 %copy-done.5 = bf16[8,16,256]{2,1,0:T(8,128)(2,1)S(1)} copy-done((bf16[8,16,256]{2,1,0:T(8,128)(2,1)S(1)}, bf16[8,16,256]{2,1,0:T(8,128)(2,1)}, u32[]{:S(2)}) %copy-start.5) | copy-done | bytes 65560
  6.6 0.0 copy-start.6
  6.6 0.8 %copy-done.6 = bf16[8,16,256]{2,1,0:T(8,128)(2,1)S(1)} copy-done((bf16[8,16,256]{2,1,0:T(8,128)(2,1)S(1)}, bf16[8,16,256]{2,1,0:T(8,128)(2,1)}, u32[]{:S(2)}) %copy-start.6) | copy-done | bytes 65560
  7.4 0.0 copy-start.7
  7.4 0.8 %copy-done.7 = bf16[8,16,256]{2,1,0:T(8,128)(2,1)S(1)} copy-done((bf16[8,16,256]{2,1,0:T(8,128)(2,1)S(1)}, bf16[8,16,256]{2,1,0:T(8,128)(2,1)}, u32[]{:S(2)}) %copy-start.7) | copy-done | bytes 65560
  8.3 0.0 copy-start.8
  8.3 0.8 %copy-done.8 = bf16[8,16,256]{2,1,0:T(8,128)(2,1)S(1)} copy-done((bf16[8,16,256]{2,1,0:T(8,128)(2,1)S(1)}, bf16[8,16,256]{2,1,0:T(8,128)(2,1)}, u32[]{:S(2)}) %copy-start.8) | copy-done | bytes 65560
  9.1 61.5 %shard_map.113 = (f32[128,256]{1,0:T(8,128)S(1)}, f32[32,10,128]{2,1,0:T(8,128)S(1)}) custom-call(bf16[8,16,256]{2,1,0:T(8,128)(2,1)S(1)} %copy-done.5, bf16[8,16,256]{2,1,0:T(8,128)(2,1)S(1)} %copy-done.6, bf16[8,16,256]{2,1,0:T(8,128)(2,1)S(1)} %copy-done.7, bf16[8,16,256]{2,1,0:T(8,128)(2,1)S(1)} %copy-done.8, f32[160,128]{1,0:T(8,128)S(1)} %copy-done, ...), custom_call_target="tpu_custom_call" | custom-call | flops 13421772800 | bytes 2097152 | tf_op jit(solution)/shard_map/pallas_call | solution.py:345
  70.6 0.7 reshape.11
  71.3 0.7 copy.13
Async XLA Ops:
  0.6 0.7 copy-start.9
  1.3 0.9 %copy-start = (f32[160,128]{1,0:T(8,128)S(1)}, f32[160,128]{1,0:T(8,128)}, u32[]{:S(2)}) copy-start(f32[160,128]{1,0:T(8,128)} %frac.1) | copy-start | bytes 245764
  2.2 0.9 %copy-start.1 = (f32[160,128]{1,0:T(8,128)S(1)}, f32[160,128]{1,0:T(8,128)}, u32[]{:S(2)}) copy-start(f32[160,128]{1,0:T(8,128)} %height.1) | copy-start | bytes 245764
  3.1 0.9 %copy-start.2 = (f32[160,128]{1,0:T(8,128)S(1)}, f32[160,128]{1,0:T(8,128)}, u32[]{:S(2)}) copy-start(f32[160,128]{1,0:T(8,128)} %noise.1) | copy-start | bytes 245764
  4.0 0.9 %copy-start.3 = (f32[160,128]{1,0:T(8,128)S(1)}, f32[160,128]{1,0:T(8,128)}, u32[]{:S(2)}) copy-start(f32[160,128]{1,0:T(8,128)} %mass.1) | copy-start | bytes 245764
  4.9 0.9 %copy-start.4 = (s32[160,128]{1,0:T(8,128)S(1)}, s32[160,128]{1,0:T(8,128)}, u32[]{:S(2)}) copy-start(s32[160,128]{1,0:T(8,128)} %column.1) | copy-start | bytes 245764
  5.8 0.8 %copy-start.5 = (bf16[8,16,256]{2,1,0:T(8,128)(2,1)S(1)}, bf16[8,16,256]{2,1,0:T(8,128)(2,1)}, u32[]{:S(2)}) copy-start(bf16[8,16,256]{2,1,0:T(8,128)(2,1)} %wind.1) | copy-start | bytes 196612
  6.6 0.8 %copy-start.6 = (bf16[8,16,256]{2,1,0:T(8,128)(2,1)S(1)}, bf16[8,16,256]{2,1,0:T(8,128)(2,1)}, u32[]{:S(2)}) copy-start(bf16[8,16,256]{2,1,0:T(8,128)(2,1)} %temp.1) | copy-start | bytes 196612
  7.4 0.8 %copy-start.7 = (bf16[8,16,256]{2,1,0:T(8,128)(2,1)S(1)}, bf16[8,16,256]{2,1,0:T(8,128)(2,1)}, u32[]{:S(2)}) copy-start(bf16[8,16,256]{2,1,0:T(8,128)(2,1)} %diff.1) | copy-start | bytes 196612
  8.3 0.8 %copy-start.8 = (bf16[8,16,256]{2,1,0:T(8,128)(2,1)S(1)}, bf16[8,16,256]{2,1,0:T(8,128)(2,1)}, u32[]{:S(2)}) copy-start(bf16[8,16,256]{2,1,0:T(8,128)(2,1)} %removal.1) | copy-start | bytes 196612

commit v2 on v1

--- a/solution.py
+++ b/solution.py
@@ -9,6 +9,7 @@
 COLS = 256
 CAP = 10
 PB = 128
+BIN = 8
 CH = 2
 F32 = jnp.float32
 BF = jnp.bfloat16
@@ -38,8 +39,8 @@
 
 def pivots(step, carry, upper_ref, lower_ref, inv_ref):
     top, bot = carry
-    for i in range(2):
-        k = 2 * step + i
+    for i in range(LEV // 2 // NG):
+        k = LEV // 2 // NG * step + i
         u = upper_ref[pl.ds(k, 1), :]
         inv = 1.0 / (top + u)
         inv_ref[pl.ds(k, 1), :] = inv
@@ -54,8 +55,60 @@
     return (top, bot), (last_top, last_bot)
 
 
-def interpolate(fr, height, col, tperm_ref, val_ref):
-    left = (1.0 - fr)
+G = 4
+NG = 8
+R = G * CAP
+
+
+def spread(x, c, rows, dtype=F32):
+    return jnp.broadcast_to(x[c:c + 1], (rows, PB)).astype(dtype)
+
+
+def move(fr, height, noise, mass, col, val, east):
+    low = jnp.clip(jnp.floor(height), 0.0, LEV - 2.0)
+    fz = height - low
+    right = fr.astype(BF).astype(F32)
+    edge = jnp.where(col == COLS - 1.0, right, 0.0)
+    low_i = low.astype(jnp.int32)
+
+    def picked(table, index):
+        return jnp.concatenate([jnp.take_along_axis(table, index[r:r + 8], axis=1) for r in range(0, R, 8)], axis=0)
+
+    w, temp, kd, rate = [
+        val[f] + edge * (picked(east[f], low_i) * (1.0 - fz) + picked(east[f], low_i + 1) * fz) for f in range(4)]
+    znew = jnp.clip(height + w + jnp.sqrt(2.0 * kd) * noise, 0.0, LEV - 1.0)
+    moved = jnp.where(mass > 0, znew, 0.0)
+    load = mass * jnp.exp(-rate) * temp
+    low = jnp.clip(jnp.floor(znew), 0.0, LEV - 2.0)
+    fz = znew - low
+    return moved, low, load * (1.0 - fz), load * fz
+
+
+def load_rows(low, load_lo, load_hi, c):
+    lev = iota((LEV, PB), 0, BF)
+    a = spread(load_lo, c, LEV, BF)
+    b = spread(load_hi, c, LEV, BF)
+    rest = jnp.where(lev == spread(low + 1.0, c, LEV, BF), b, jnp.zeros_like(b))
+    return jnp.where(lev == spread(low, c, LEV, BF), a, rest)
+
+
+def pick_rows(col, c):
+    one = jnp.ones((COLS, PB), BF)
+    return jnp.where(iota((COLS, PB), 0, BF) == spread(col, c, COLS, BF), one, jnp.zeros_like(one))
+
+
+def bin_part(low, load_lo, load_hi, col, rows):
+    picks = jnp.concatenate([pick_rows(col, c) for c in rows], axis=1)
+    loads = jnp.concatenate([load_rows(low, load_lo, load_hi, c) for c in rows], axis=1)
+    return lax.dot_general(picks, loads, (((1,), (1,)), ((), ())), preferred_element_type=F32)
+
+
+def group_work(now, before, tperm_ref, val_ref, east):
+    fr, height, col = now
+    if before is not None:
+        moved, b_low, b_lo, b_hi = move(*before, east)
+        b_col = before[4]
+    left = 1.0 - fr
     low = jnp.clip(jnp.floor(height), 0.0, LEV - 2.0)
     odd_i = jnp.floor(low * 0.5)
     even_i = jnp.floor((low + 1.0) * 0.5)
@@ -65,21 +118,16 @@
     g_odd = jnp.floor(odd_i * 0.125)
     s_even = even_i - 8.0 * g_even
     s_odd = odd_i - 8.0 * g_odd
+    col1 = col + 1.0
     ids = iota((COLS, PB), 0, BF)
     sub = iota((8, PB), 0)
     zero = jnp.zeros((COLS, PB), BF)
-
-    def spread(x, c, rows, dtype=F32):
-        return jnp.broadcast_to(x[c:c + 1], (rows, PB)).astype(dtype)
-
-    for c0 in range(0, CAP, CH):
+    bins = None
+    for c0 in range(0, R, CH):
         weights = []
         for c in range(c0, c0 + CH):
-            cb = spread(col, c, COLS, BF)
-            cb1 = spread(col + 1.0, c, COLS, BF)
-            lb = spread(left, c, COLS, BF)
-            rb = spread(fr, c, COLS, BF)
-            weights.append(jnp.where(ids == cb, lb, jnp.where(ids == cb1, rb, zero)))
+            rest = jnp.where(ids == spread(col1, c, COLS, BF), spread(fr, c, COLS, BF), zero)
+            weights.append(jnp.where(ids == spread(col, c, COLS, BF), spread(left, c, COLS, BF), rest))
         horiz = jnp.dot(tperm_ref[...], jnp.concatenate(weights, axis=1), preferred_element_type=F32)
         for i in range(CH):
             c = c0 + i
@@ -98,45 +146,16 @@
                     e = jnp.where(e_masks[g - 1], horiz[base + 8 * g:base + 8 * g + 8, lanes], e)
                     o = jnp.where(o_masks[g - 1], horiz[base + 64 + 8 * g:base + 72 + 8 * g, lanes], o)
                 val_ref[f, c:c + 1, :] = jnp.sum(e * we + o * wo, axis=0, keepdims=True)
-
-
-def move(fr, height, noise, mass, col, val, east):
-    low = jnp.clip(jnp.floor(height), 0.0, LEV - 2.0)
-    fz = height - low
-    right = fr.astype(BF).astype(F32)
-    edge = jnp.where(col == COLS - 1.0, right, 0.0)
-    low_i = low.astype(jnp.int32)
-    pad = jnp.zeros((16 - CAP, PB), jnp.int32)
-    low_p = jnp.concatenate([low_i, pad], axis=0)
-    out = []
-    for f in range(4):
-        lo = jnp.concatenate([jnp.take_along_axis(east[f], low_p[r:r + 8], axis=1) for r in (0, 8)], axis=0)[:CAP]
-        hi = jnp.concatenate([jnp.take_along_axis(east[f], low_p[r:r + 8] + 1, axis=1) for r in (0, 8)], axis=0)[:CAP]
-        out.append(val[f] + edge * (lo * (1.0 - fz) + hi * fz))
-    w, temp, kd, rate = out
-    znew = jnp.clip(height + w + jnp.sqrt(2.0 * kd) * noise, 0.0, LEV - 1.0)
-    moved = jnp.where(mass > 0, znew, 0.0)
-    load = mass * jnp.exp(-rate) * temp
-    low = jnp.clip(jnp.floor(znew), 0.0, LEV - 2.0)
-    fz = znew - low
-    return moved, low, load * (1.0 - fz), load * fz
-
-
-def binning(low, load_lo, load_hi, col):
-    lev = iota((LEV, PB), 0, BF)
-    ids = iota((COLS, PB), 0, BF)
-    one = jnp.ones((COLS, PB), BF)
-    loads, picks = [], []
-    for c in range(CAP):
-        lb = jnp.broadcast_to(low[c:c + 1], (LEV, PB)).astype(BF)
-        hb = jnp.broadcast_to(low[c:c + 1] + 1.0, (LEV, PB)).astype(BF)
-        a = jnp.broadcast_to(load_lo[c:c + 1], (LEV, PB)).astype(BF)
-        b = jnp.broadcast_to(load_hi[c:c + 1], (LEV, PB)).astype(BF)
-        loads.append(jnp.where(lev == lb, a, jnp.where(lev == hb, b, jnp.zeros_like(a))))
-        cb = jnp.broadcast_to(col[c:c + 1], (COLS, PB)).astype(BF)
-        picks.append(jnp.where(ids == cb, one, jnp.zeros_like(one)))
-    return lax.dot_general(jnp.concatenate(picks, axis=1), jnp.concatenate(loads, axis=1),
-                           (((1,), (1,)), ((), ())), preferred_element_type=F32)
+        if before is not None and (c0 + CH) % BIN == 0:
+            part = bin_part(b_low, b_lo, b_hi, b_col, range(c0 + CH - BIN, c0 + CH))
+            bins = part if bins is None else bins + part
+    if before is not None:
+        return moved, bins
+
+
+def last_group(before, east):
+    moved, low, lo, hi = move(*before, east)
+    return moved, bin_part(low, lo, hi, before[4], range(R))
 
 
 def solve(ends, binned, upper_ref, lower_ref, inv_ref, rhs_ref, fwd_ref, back_ref, out_ref):
@@ -222,8 +241,8 @@
 def kernel(wind, temp, diff, removal, frac, height, noise, mass, column, dest,
            conc_ref, moved_ref,
            table, tperm, east_out, east_in, send_f, send_c, recv_f, recv_c,
-           val, binned, upper, lower, inv, rhs, fwd, back,
-           field_send, field_recv, own_sem, east_sems, f_send, f_recv, c_send, c_recv):
+           in_f, in_c, in_d, val, val_old, binned, upper, lower, inv, rhs, fwd, back,
+           field_send, field_recv, own_sem, in_sem, east_sems, f_send, f_recv, c_send, c_recv):
     band, tile = lax.axis_index("band"), lax.axis_index("tile")
     barrier = pltpu.get_barrier_semaphore()
 
@@ -235,6 +254,11 @@
         pl.semaphore_signal(barrier, inc=1, device_id=((band + i) % N_BAND, tile), device_id_type=pl.DeviceIdType.MESH)
         return 0
 
+    loads = [pltpu.make_async_copy(ref, in_f.at[f], in_sem.at[f]) for f, ref in enumerate((frac, height, noise, mass))]
+    loads.append(pltpu.make_async_copy(column, in_c, in_sem.at[4]))
+    loads.append(pltpu.make_async_copy(dest, in_d, in_sem.at[5]))
+    for copy in loads:
+        copy.start()
     lax.fori_loop(1, N_TILE, greet_tile, 0)
     lax.fori_loop(1, N_BAND, greet_band, 0)
     fields = (wind, temp, diff, removal)
@@ -242,7 +266,9 @@
            for f, ref in enumerate(fields)]
     for copy in own:
         copy.start()
-    build(dest, (frac, height, noise, mass), column, send_f, send_c)
+    for copy in loads:
+        copy.wait()
+    build(in_d, [in_f.at[f] for f in range(4)], in_c, send_f, send_c)
     pl.semaphore_wait(barrier, N_TILE + N_BAND - 2)
 
     def field_copy(i, f, to, rows_of):
@@ -251,13 +277,14 @@
             send_sem=field_send.at[i, f], recv_sem=field_recv.at[i, f],
             device_id=(to, tile), device_id_type=pl.DeviceIdType.MESH)
 
-    def record_copies(i, to, slot):
+    def record_copies(i):
+        to = place(tile, i, 1)
         return [pltpu.make_async_remote_copy(
-            src_ref=send_f.at[pl.ds(pl.multiple_of(to * ROWS, 8), ROWS)], dst_ref=recv_f.at[slot],
+            src_ref=send_f.at[pl.ds(pl.multiple_of(to * ROWS, 8), ROWS)], dst_ref=recv_f.at[i // G, pl.ds(pl.multiple_of(i % G * ROWS, 8), ROWS)],
             send_sem=f_send.at[i], recv_sem=f_recv.at[i],
             device_id=(band, to), device_id_type=pl.DeviceIdType.MESH),
             pltpu.make_async_remote_copy(
-            src_ref=send_c.at[to], dst_ref=recv_c.at[slot],
+            src_ref=send_c.at[to], dst_ref=recv_c.at[i],
             send_sem=c_send.at[i], recv_sem=c_recv.at[i],
             device_id=(band, to), device_id_type=pl.DeviceIdType.MESH)]
 
@@ -268,14 +295,14 @@
         return 0
 
     def send_records(i, _):
-        for copy in record_copies(i, place(tile, i, 1), tile):
+        for copy in record_copies(i):
             copy.start()
         return 0
 
     lax.fori_loop(1, N_BAND, send_fields, 0)
     lax.fori_loop(1, N_TILE, send_records, 0)
-    recv_f[tile] = send_f[pl.ds(pl.multiple_of(tile * ROWS, 8), ROWS), :]
-    recv_c[tile] = send_c[tile]
+    recv_f[0, 0:ROWS, :] = send_f[pl.ds(pl.multiple_of(tile * ROWS, 8), ROWS), :]
+    recv_c[0] = send_c[tile]
     binned[...] = jnp.zeros_like(binned)
     for copy in own:
         copy.wait()
@@ -296,32 +323,46 @@
     east_copy.start()
     split_levels(table, tperm)
     set_kappa(table, upper, lower)
+    def take_records(i, _):
+        for copy in record_copies(i):
+            copy.wait_recv()
+        return 0
+
+    def rows_of(q):
+        return [recv_f[q, pl.ds(f, R, stride=4), :] for f in range(4)]
+
+    def col_of(q):
+        return jnp.concatenate([recv_c[q * G + j].astype(F32)[:CAP] for j in range(G)], axis=0)
+
+    def before_of(q):
+        return (*rows_of(q), col_of(q), [val_old[f] for f in range(4)])
+
+    def put(q, moved):
+        for j in range(G):
+            moved_ref[place(tile, q * G + j, -1)] = moved[j * CAP:(j + 1) * CAP]
+
+    lax.fori_loop(1, G, take_records, 0)
+    one = jnp.ones((1, COLS), F32)
+    carry = pivots(0, (one, one), upper, lower, inv)
+    fr, h, _, _ = rows_of(0)
+    group_work((fr, h, col_of(0)), None, tperm, val_old, None)
     east_copy.wait()
-
-    def body(i, carry):
-        source = place(tile, i, -1)
-
-        @pl.when(i > 0)
-        def _():
-            for copy in record_copies(i, place(tile, i, 1), source):
-                copy.wait_recv()
-
-        carry, ends = pivots(i, carry[0], upper, lower, inv)
-        fr = recv_f[source, pl.ds(0, CAP, stride=4), :]
-        h = recv_f[source, pl.ds(1, CAP, stride=4), :]
-        n = recv_f[source, pl.ds(2, CAP, stride=4), :]
-        m = recv_f[source, pl.ds(3, CAP, stride=4), :]
-        col = recv_c[source].astype(F32)[:CAP]
-        interpolate(fr, h, col, tperm, val)
-        east = [east_in[:, f * LEV:(f + 1) * LEV] for f in range(4)]
-        moved, low, a, b = move(fr, h, n, m, col, [val[f, 0:CAP, :] for f in range(4)], east)
-        moved_ref[source] = moved
-        binned[...] += binning(low, a, b, col)
+    east = [east_in[:, f * LEV:(f + 1) * LEV] for f in range(4)]
+
+    def body(q, carry):
+        lax.fori_loop(q * G, q * G + G, take_records, 0)
+        carry, ends = pivots(q, carry[0], upper, lower, inv)
+        fr, h, _, _ = rows_of(q)
+        moved, bins = group_work((fr, h, col_of(q)), before_of(q - 1), tperm, val, east)
+        put(q - 1, moved)
+        binned[...] += bins
+        val_old[...] = val[...]
         return carry, ends
 
-    one = jnp.ones((1, COLS), F32)
-    _, ends = lax.fori_loop(0, N_TILE, body, ((one, one), (one, one)))
-    solve(ends, binned[...].T, upper, lower, inv, rhs, fwd, back, conc_ref)
+    _, ends = lax.fori_loop(1, NG, body, carry)
+    moved, bins = last_group(before_of(NG - 1), east)
+    put(NG - 1, moved)
+    solve(ends, (binned[...] + bins).T, upper, lower, inv, rhs, fwd, back, conc_ref)
 
     def sent_fields(i, _):
         for f in range(4):
@@ -329,7 +370,7 @@
         return 0
 
     def sent_records(i, _):
-        for copy in record_copies(i, place(tile, i, 1), tile):
+        for copy in record_copies(i):
             copy.wait_send()
         return 0
 
@@ -339,26 +380,27 @@
 
 def shards(wind, temp, diff, removal, frac, height, mass, noise, column, dest):
     vm = pl.BlockSpec(memory_space=pltpu.VMEM)
-    hbm = pl.BlockSpec(memory_space=pl.ANY)
+    hbm = pl.BlockSpec(memory_space=pltpu.HBM)
     grid = pltpu.VMEM((LEV, COLS), F32)
     dma = pltpu.SemaphoreType.DMA
     conc, moved = pl.pallas_call(
         kernel,
         out_shape=(jax.ShapeDtypeStruct((LEV, COLS), F32), jax.ShapeDtypeStruct((N_TILE, CAP, PB), F32)),
-        in_specs=[hbm] * 4 + [vm] * 6,
+        in_specs=[hbm] * 10,
         out_specs=(vm, vm),
         scratch_shapes=[
             pltpu.VMEM((4 * LEV, COLS), BF), pltpu.VMEM((4 * LEV, COLS), BF),
             pltpu.VMEM((8, 4 * LEV), F32), pltpu.VMEM((8, 4 * LEV), F32),
             pltpu.VMEM((N_TILE * ROWS, PB), F32), pltpu.VMEM((N_TILE, 16, PB), BF),
-            pltpu.VMEM((N_TILE, ROWS, PB), F32), pltpu.VMEM((N_TILE, 16, PB), BF),
-            pltpu.VMEM((4, 16, PB), F32), pltpu.VMEM((COLS, LEV), F32),
+            pltpu.VMEM((NG, G * ROWS, PB), F32), pltpu.VMEM((N_TILE, 16, PB), BF),
+            pltpu.VMEM((4, B_DEV, PB), F32), pltpu.VMEM((B_DEV, PB), jnp.int32), pltpu.VMEM((1, B_DEV), jnp.int32),
+            pltpu.VMEM((4, R, PB), F32), pltpu.VMEM((4, R, PB), F32), pltpu.VMEM((COLS, LEV), F32),
             grid, grid, grid, grid, grid, grid,
-            dma((N_BAND, 4)), dma((N_BAND, 4)), dma((4,)), dma((2,)),
+            dma((N_BAND, 4)), dma((N_BAND, 4)), dma((4,)), dma((6,)), dma((2,)),
             dma((N_TILE,)), dma((N_TILE,)), dma((N_TILE,)), dma((N_TILE,)),
         ],
         compiler_params=pltpu.CompilerParams(
-            collective_id=0, has_side_effects=True, vmem_limit_bytes=48 * 2**20),
+            collective_id=0, has_side_effects=True, vmem_limit_bytes=63 * 2**20),
         cost_estimate=pl.CostEstimate(flops=2 * 40960 * 256 * 640, bytes_accessed=2 * 2**20, transcendentals=0),
     )(wind, temp, diff, removal, frac, height, noise, mass, column, dest.reshape(1, B_DEV))
     return conc[None], moved.reshape(N_TILE * CAP, PB)

time: 72.7 us -> 54.3 us (0.75)
  Pallas kernels: 61.5 us -> 50.8 us
  local copies, waits for them, and re-layouts: 9.8 us -> 2.33 us
    pallas_call x1, Pallas kernels: 61.5 us -> 50.8 us  [shards(): pl.pallas_call(kernel, out_shape=(jax.ShapeDtypeStruct((LEV, COLS), F32),...]
    unnamed x21 -> x3, local copies, waits for them, and re-layouts: 9.11 us -> 0.66 us
    reshape x1, local copies, waits for them, and re-layouts: 0.68 us -> 1.67 us  [shards(): return (conc[None], moved.reshape(N_TILE * CAP, PB))]
where the time goes in v2:
time: 54.3 us; the launch traced here: 53.8 us
  Pallas kernels  50.8 us (94%)
  local copies, waits for them, and re-layouts  2.33 us (4%)
  between operations  0.65 us (1%)
    pallas_call x1, Pallas kernels, shards(): pl.pallas_call(kernel, out_shape=(jax.ShapeDtypeStruct((LEV, COLS), F32),...  50.8 us
    reshape x1, local copies, waits for them, and re-layouts, shards(): return (conc[None], moved.reshape(N_TILE * CAP, PB))  1.67 us

profile of v2, /device:TPU:1, one launch (start us, length us, event | category | flops | bytes accessed | tf_op | source)
XLA Modules:
  0.0 53.8 jit_solution(12655757551980632727)
XLA Ops:
  0.6 50.8 %shard_map.113 = (f32[128,256]{1,0:T(8,128)}, f32[32,10,128]{2,1,0:T(8,128)}) custom-call(bf16[8,16,256]{2,1,0:T(8,128)(2,1)} %wind.1, bf16[8,16,256]{2,1,0:T(8,128)(2,1)} %temp.1, bf16[8,16,256]{2,1,0:T(8,128)(2,1)} %diff.1, bf16[8,16,256]{2,1,0:T(8,128)(2,1)} %removal.1, f32[160,128]{1,0:T(8,128)} %frac.1, f32[160,128]{1,0:T(8,128)} %height.1, ...), custom_call_target="tpu_custom_call" | custom-call | flops 13421772800 | bytes 2097152 | tf_op jit(solution)/shard_map/pallas_call | solution.py:386
  51.5 0.0 copy-start
  51.5 1.7 %reshape.11 = f32[320,128]{1,0:T(8,128)} reshape(f32[32,10,128]{2,1,0:T(8,128)} %get-tuple-element.5) | data formatting | bytes 327680 | tf_op jit(solution)/shard_map/reshape | solution.py:406
  53.2 0.0 copy-done
  53.2 0.7 %copy.13 = f32[1,128,256]{2,1,0:T(8,128)} copy(f32[1,128,256]{2,1,0:T(8,128)S(1)} %bitcast.2) | data formatting | bytes 262144
Async XLA Ops:
  51.5 1.7 %copy-start = (f32[128,256]{1,0:T(8,128)S(1)}, f32[128,256]{1,0:T(8,128)}, u32[]{:S(2)}) copy-start(f32[128,256]{1,0:T(8,128)} %get-tuple-element.4) | copy-start | bytes 393220

commit v3 on v2

--- a/solution.py
+++ b/solution.py
@@ -9,7 +9,6 @@
 COLS = 256
 CAP = 10
 PB = 128
-BIN = 8
 CH = 2
 F32 = jnp.float32
 BF = jnp.bfloat16
@@ -92,22 +91,21 @@
     return jnp.where(lev == spread(low, c, LEV, BF), a, rest)
 
 
-def pick_rows(col, c):
-    one = jnp.ones((COLS, PB), BF)
-    return jnp.where(iota((COLS, PB), 0, BF) == spread(col, c, COLS, BF), one, jnp.zeros_like(one))
-
-
-def bin_part(low, load_lo, load_hi, col, rows):
-    picks = jnp.concatenate([pick_rows(col, c) for c in rows], axis=1)
-    loads = jnp.concatenate([load_rows(low, load_lo, load_hi, c) for c in rows], axis=1)
-    return lax.dot_general(picks, loads, (((1,), (1,)), ((), ())), preferred_element_type=F32)
+def bin_rows(low, load_lo, load_hi, col):
+    loads = jnp.concatenate([load_rows(low, load_lo, load_hi, c) for c in range(R)], axis=1)
+    turned = jnp.concatenate([col, jnp.zeros((PB - R, PB), F32)], axis=0).T.astype(BF)
+    lanes = iota((PB, COLS), 1, BF)
+    one = jnp.ones((PB, COLS), BF)
+    picks = jnp.concatenate(
+        [jnp.where(lanes == jnp.broadcast_to(turned[:, c:c + 1], (PB, COLS)), one, jnp.zeros_like(one)) for c in range(R)],
+        axis=0)
+    return jnp.dot(loads, picks, preferred_element_type=F32)
 
 
 def group_work(now, before, tperm_ref, val_ref, east):
     fr, height, col = now
     if before is not None:
         moved, b_low, b_lo, b_hi = move(*before, east)
-        b_col = before[4]
     left = 1.0 - fr
     low = jnp.clip(jnp.floor(height), 0.0, LEV - 2.0)
     odd_i = jnp.floor(low * 0.5)
@@ -122,7 +120,6 @@
     ids = iota((COLS, PB), 0, BF)
     sub = iota((8, PB), 0)
     zero = jnp.zeros((COLS, PB), BF)
-    bins = None
     for c0 in range(0, R, CH):
         weights = []
         for c in range(c0, c0 + CH):
@@ -146,16 +143,13 @@
                     e = jnp.where(e_masks[g - 1], horiz[base + 8 * g:base + 8 * g + 8, lanes], e)
                     o = jnp.where(o_masks[g - 1], horiz[base + 64 + 8 * g:base + 72 + 8 * g, lanes], o)
                 val_ref[f, c:c + 1, :] = jnp.sum(e * we + o * wo, axis=0, keepdims=True)
-        if before is not None and (c0 + CH) % BIN == 0:
-            part = bin_part(b_low, b_lo, b_hi, b_col, range(c0 + CH - BIN, c0 + CH))
-            bins = part if bins is None else bins + part
     if before is not None:
-        return moved, bins
+        return moved, bin_rows(b_low, b_lo, b_hi, before[4])
 
 
 def last_group(before, east):
     moved, low, lo, hi = move(*before, east)
-    return moved, bin_part(low, lo, hi, before[4], range(R))
+    return moved, bin_rows(low, lo, hi, before[4])
 
 
 def solve(ends, binned, upper_ref, lower_ref, inv_ref, rhs_ref, fwd_ref, back_ref, out_ref):
@@ -196,13 +190,18 @@
 N_TILE = 32
 NY, NZ = 4, 8
 B_DEV = 160
+AHEAD = 5
 SUB = LEV // N_BAND
 ROWS = 4 * CAP
 
 
 def offset(i):
-    q, dy = i // NY, i % NY
-    dz = ((q + 1) // 2) * (q % 2) + ((NZ - q // 2) % NZ) * (1 - q % 2)
+    j = (i + NY) // (2 * NY)
+    r = (i + NY) % (2 * NY)
+    dy = (1 - (j + 7) // 8) * (r % NY) + ((j + 7) // 8) * (r // 2)
+    dz = (j + (r % 2) * (NZ - 2 * j)) % NZ
+    dz = dz * (1 - j // 4) + 4 * (j // 4)
+    dy = dy * (1 - j // 4) + (j // 4) * (r % NY)
     return dy, dz
 
 
@@ -266,9 +265,6 @@
            for f, ref in enumerate(fields)]
     for copy in own:
         copy.start()
-    for copy in loads:
-        copy.wait()
-    build(in_d, [in_f.at[f] for f in range(4)], in_c, send_f, send_c)
     pl.semaphore_wait(barrier, N_TILE + N_BAND - 2)
 
     def field_copy(i, f, to, rows_of):
@@ -300,7 +296,10 @@
         return 0
 
     lax.fori_loop(1, N_BAND, send_fields, 0)
-    lax.fori_loop(1, N_TILE, send_records, 0)
+    for copy in loads:
+        copy.wait()
+    build(in_d, [in_f.at[f] for f in range(4)], in_c, send_f, send_c)
+    lax.fori_loop(1, AHEAD * G, send_records, 0)
     recv_f[0, 0:ROWS, :] = send_f[pl.ds(pl.multiple_of(tile * ROWS, 8), ROWS), :]
     recv_c[0] = send_c[tile]
     binned[...] = jnp.zeros_like(binned)
@@ -339,7 +338,7 @@
 
     def put(q, moved):
         for j in range(G):
-            moved_ref[place(tile, q * G + j, -1)] = moved[j * CAP:(j + 1) * CAP]
+            moved_ref[pl.ds(place(tile, q * G + j, -1) * CAP, CAP), :] = moved[j * CAP:(j + 1) * CAP]
 
     lax.fori_loop(1, G, take_records, 0)
     one = jnp.ones((1, COLS), F32)
@@ -351,6 +350,8 @@
 
     def body(q, carry):
         lax.fori_loop(q * G, q * G + G, take_records, 0)
+        first = jnp.minimum((q + AHEAD - 1) * G, N_TILE)
+        lax.fori_loop(first, jnp.minimum(first + G, N_TILE), send_records, 0)
         carry, ends = pivots(q, carry[0], upper, lower, inv)
         fr, h, _, _ = rows_of(q)
         moved, bins = group_work((fr, h, col_of(q)), before_of(q - 1), tperm, val, east)
@@ -362,7 +363,7 @@
     _, ends = lax.fori_loop(1, NG, body, carry)
     moved, bins = last_group(before_of(NG - 1), east)
     put(NG - 1, moved)
-    solve(ends, (binned[...] + bins).T, upper, lower, inv, rhs, fwd, back, conc_ref)
+    solve(ends, binned[...] + bins, upper, lower, inv, rhs, fwd, back, conc_ref)
 
     def sent_fields(i, _):
         for f in range(4):
@@ -385,7 +386,7 @@
     dma = pltpu.SemaphoreType.DMA
     conc, moved = pl.pallas_call(
         kernel,
-        out_shape=(jax.ShapeDtypeStruct((LEV, COLS), F32), jax.ShapeDtypeStruct((N_TILE, CAP, PB), F32)),
+        out_shape=(jax.ShapeDtypeStruct((LEV, COLS), F32), jax.ShapeDtypeStruct((N_TILE * CAP, PB), F32)),
         in_specs=[hbm] * 10,
         out_specs=(vm, vm),
         scratch_shapes=[
@@ -394,7 +395,7 @@
             pltpu.VMEM((N_TILE * ROWS, PB), F32), pltpu.VMEM((N_TILE, 16, PB), BF),
             pltpu.VMEM((NG, G * ROWS, PB), F32), pltpu.VMEM((N_TILE, 16, PB), BF),
             pltpu.VMEM((4, B_DEV, PB), F32), pltpu.VMEM((B_DEV, PB), jnp.int32), pltpu.VMEM((1, B_DEV), jnp.int32),
-            pltpu.VMEM((4, R, PB), F32), pltpu.VMEM((4, R, PB), F32), pltpu.VMEM((COLS, LEV), F32),
+            pltpu.VMEM((4, R, PB), F32), pltpu.VMEM((4, R, PB), F32), grid,
             grid, grid, grid, grid, grid, grid,
             dma((N_BAND, 4)), dma((N_BAND, 4)), dma((4,)), dma((6,)), dma((2,)),
             dma((N_TILE,)), dma((N_TILE,)), dma((N_TILE,)), dma((N_TILE,)),
@@ -403,7 +404,7 @@
             collective_id=0, has_side_effects=True, vmem_limit_bytes=63 * 2**20),
         cost_estimate=pl.CostEstimate(flops=2 * 40960 * 256 * 640, bytes_accessed=2 * 2**20, transcendentals=0),
     )(wind, temp, diff, removal, frac, height, noise, mass, column, dest.reshape(1, B_DEV))
-    return conc[None], moved.reshape(N_TILE * CAP, PB)
+    return conc[None], moved
 
 
 def solution(mesh):

time: 54.3 us -> 46.1 us (0.85)
  the two profiles are of different devices: /device:TPU:1 before, /device:TPU:66 now
where the time goes in v3:
time: 46.1 us; the launch traced here: 46 us
  Pallas kernels  43.1 us (93%)
  local copies, waits for them, and re-layouts  2.28 us (5%)
  between operations  0.65 us (1%)
    pallas_call x1, Pallas kernels, shards(): pl.pallas_call(kernel, out_shape=(jax.ShapeDtypeStruct((LEV, COLS), F32),...  43.1 us
    unnamed x4, local copies, waits for them, and re-layouts  2.28 us

profile of v3, /device:TPU:66, one launch (start us, length us, event | category | flops | bytes accessed | tf_op | source)
XLA Modules:
  0.0 46.0 jit_solution(730111784322387899)
XLA Ops:
  0.6 43.1 %shard_map.113 = (f32[128,256]{1,0:T(8,128)}, f32[320,128]{1,0:T(8,128)}) custom-call(bf16[8,16,256]{2,1,0:T(8,128)(2,1)} %wind.1, bf16[8,16,256]{2,1,0:T(8,128)(2,1)} %temp.1, bf16[8,16,256]{2,1,0:T(8,128)(2,1)} %diff.1, bf16[8,16,256]{2,1,0:T(8,128)(2,1)} %removal.1, f32[160,128]{1,0:T(8,128)} %frac.1, f32[160,128]{1,0:T(8,128)} %height.1, ...), custom_call_target="tpu_custom_call" | custom-call | flops 13421772800 | bytes 2097152 | tf_op jit(solution)/shard_map/pallas_call | solution.py:387
  43.7 0.0 copy-start
  43.7 1.6 %copy.14 = f32[1,128,256]{2,1,0:T(8,128)} copy(f32[1,128,256]{2,1,0:T(8,128)} %bitcast.2) | data formatting | bytes 262144
  45.3 0.0 copy-done
  45.3 0.7 %copy.15 = f32[320,128]{1,0:T(8,128)} copy(f32[320,128]{1,0:T(8,128)S(1)} %copy-done) | data formatting | bytes 327680
Async XLA Ops:
  43.7 1.6 %copy-start = (f32[320,128]{1,0:T(8,128)S(1)}, f32[320,128]{1,0:T(8,128)}, u32[]{:S(2)}) copy-start(f32[320,128]{1,0:T(8,128)} %get-tuple-element.9) | copy-start | bytes 491524

commit v4 on v3

--- a/solution.py
+++ b/solution.py
@@ -192,7 +192,7 @@
 B_DEV = 160
 AHEAD = 5
 SUB = LEV // N_BAND
-ROWS = 4 * CAP
+ROWS = 32
 
 
 def offset(i):
@@ -222,7 +222,7 @@
     rank = jnp.sum(same, axis=0, keepdims=True)
     slots = N_TILE * CAP
     pick = jnp.where(iota((slots, B_DEV), 0) == dest * CAP + rank, 1.0, 0.0).astype(BF)
-    for f, ref in enumerate(parts):
+    for f, ref in enumerate(parts[:3]):
         x = ref[...]
         hi = x.astype(BF)
         rest = x - hi.astype(F32)
@@ -231,10 +231,21 @@
         total = jnp.dot(pick, hi, preferred_element_type=F32)
         total = total + jnp.dot(pick, mid, preferred_element_type=F32)
         total = total + jnp.dot(pick, low, preferred_element_type=F32)
-        send_f[pl.ds(f, slots, stride=4), :] = total
-    pick = jnp.where(iota((N_TILE * 16, B_DEV), 0) == dest * 16 + rank, 1.0, 0.0).astype(BF)
-    cols = jnp.dot(pick, col_ref[...].astype(F32).astype(BF), preferred_element_type=F32)
-    send_c[...] = cols.astype(BF).reshape(N_TILE, 16, PB)
+        for t in range(N_TILE):
+            send_f[t * ROWS + f * CAP:t * ROWS + (f + 1) * CAP, :] = total[t * CAP:(t + 1) * CAP]
+    mass = parts[3][...].astype(BF)
+    total = jnp.dot(pick, mass, preferred_element_type=F32)
+    for t in range(N_TILE):
+        for r in range(2):
+            at = t * CAP + 6 + 2 * r
+            send_f[t * ROWS + 30 + r:t * ROWS + 31 + r, :] = total[at:at + 1] * 1024.0 + total[at + 1:at + 2]
+    rows = iota((N_TILE * 16, B_DEV), 0)
+    place16 = dest * 16 + rank
+    pick = jnp.where(rows == place16, 1.0, 0.0).astype(BF)
+    both = jnp.dot(pick, col_ref[...].astype(F32).astype(BF), preferred_element_type=F32)
+    pick = jnp.where(rows == jnp.where(rank < 6.0, place16 + 10.0, -1.0), 1.0, 0.0).astype(BF)
+    both = both + jnp.dot(pick, mass, preferred_element_type=F32)
+    send_c[...] = both.astype(BF).reshape(N_TILE, 16, PB)
 
 
 def kernel(wind, temp, diff, removal, frac, height, noise, mass, column, dest,
@@ -265,6 +276,9 @@
            for f, ref in enumerate(fields)]
     for copy in own:
         copy.start()
+    for copy in loads:
+        copy.wait()
+    build(in_d, [in_f.at[f] for f in range(4)], in_c, send_f, send_c)
     pl.semaphore_wait(barrier, N_TILE + N_BAND - 2)
 
     def field_copy(i, f, to, rows_of):
@@ -295,11 +309,8 @@
             copy.start()
         return 0
 
+    lax.fori_loop(1, AHEAD * G, send_records, 0)
     lax.fori_loop(1, N_BAND, send_fields, 0)
-    for copy in loads:
-        copy.wait()
-    build(in_d, [in_f.at[f] for f in range(4)], in_c, send_f, send_c)
-    lax.fori_loop(1, AHEAD * G, send_records, 0)
     recv_f[0, 0:ROWS, :] = send_f[pl.ds(pl.multiple_of(tile * ROWS, 8), ROWS), :]
     recv_c[0] = send_c[tile]
     binned[...] = jnp.zeros_like(binned)
@@ -328,13 +339,24 @@
         return 0
 
     def rows_of(q):
-        return [recv_f[q, pl.ds(f, R, stride=4), :] for f in range(4)]
+        return [jnp.concatenate([recv_f[q, j * ROWS + f * CAP:j * ROWS + (f + 1) * CAP, :] for j in range(G)], axis=0)
+                for f in range(3)]
 
     def col_of(q):
         return jnp.concatenate([recv_c[q * G + j].astype(F32)[:CAP] for j in range(G)], axis=0)
 
+    def mass_of(q):
+        out = []
+        for j in range(G):
+            out.append(recv_c[q * G + j].astype(F32)[CAP:])
+            for r in range(2):
+                pair = recv_f[q, j * ROWS + 30 + r:j * ROWS + 31 + r, :]
+                even = jnp.floor(pair * 0.25) * (1.0 / 256.0)
+                out += [even, pair - even * 1024.0]
+        return jnp.concatenate(out, axis=0)
+
     def before_of(q):
-        return (*rows_of(q), col_of(q), [val_old[f] for f in range(4)])
+        return (*rows_of(q), mass_of(q), col_of(q), [val_old[f] for f in range(4)])
 
     def put(q, moved):
         for j in range(G):
@@ -343,7 +365,7 @@
     lax.fori_loop(1, G, take_records, 0)
     one = jnp.ones((1, COLS), F32)
     carry = pivots(0, (one, one), upper, lower, inv)
-    fr, h, _, _ = rows_of(0)
+    fr, h, _ = rows_of(0)
     group_work((fr, h, col_of(0)), None, tperm, val_old, None)
     east_copy.wait()
     east = [east_in[:, f * LEV:(f + 1) * LEV] for f in range(4)]
@@ -353,7 +375,7 @@
         first = jnp.minimum((q + AHEAD - 1) * G, N_TILE)
         lax.fori_loop(first, jnp.minimum(first + G, N_TILE), send_records, 0)
         carry, ends = pivots(q, carry[0], upper, lower, inv)
-        fr, h, _, _ = rows_of(q)
+        fr, h, _ = rows_of(q)
         moved, bins = group_work((fr, h, col_of(q)), before_of(q - 1), tperm, val, east)
         put(q - 1, moved)
         binned[...] += bins

time: 46.1 us -> 44.1 us (0.957)
  the two profiles are of different devices: /device:TPU:66 before, /device:TPU:1 now
where the time goes in v4:
time: 44.1 us; the launch traced here: 44 us
  Pallas kernels  41.1 us (93%)
  local copies, waits for them, and re-layouts  2.28 us (5%)
  between operations  0.65 us (1%)
    pallas_call x1, Pallas kernels, shards(): pl.pallas_call(kernel, out_shape=(jax.ShapeDtypeStruct((LEV, COLS), F32),...  41.1 us
    unnamed x4, local copies, waits for them, and re-layouts  2.28 us

profile of v4, /device:TPU:1, one launch (start us, length us, event | category | flops | bytes accessed | tf_op | source)
XLA Modules:
  0.0 44.0 jit_solution(15132808841515124895)
XLA Ops:
  0.6 41.1 %shard_map.113 = (f32[128,256]{1,0:T(8,128)}, f32[320,128]{1,0:T(8,128)}) custom-call(bf16[8,16,256]{2,1,0:T(8,128)(2,1)} %wind.1, bf16[8,16,256]{2,1,0:T(8,128)(2,1)} %temp.1, bf16[8,16,256]{2,1,0:T(8,128)(2,1)} %diff.1, bf16[8,16,256]{2,1,0:T(8,128)(2,1)} %removal.1, f32[160,128]{1,0:T(8,128)} %frac.1, f32[160,128]{1,0:T(8,128)} %height.1, ...), custom_call_target="tpu_custom_call" | custom-call | flops 13421772800 | bytes 2097152 | tf_op jit(solution)/shard_map/pallas_call | solution.py:409
  41.8 0.0 copy-start
  41.8 1.6 %copy.14 = f32[1,128,256]{2,1,0:T(8,128)} copy(f32[1,128,256]{2,1,0:T(8,128)} %bitcast.2) | data formatting | bytes 262144
  43.4 0.0 copy-done
  43.4 0.7 %copy.15 = f32[320,128]{1,0:T(8,128)} copy(f32[320,128]{1,0:T(8,128)S(1)} %copy-done) | data formatting | bytes 327680
Async XLA Ops:
  41.8 1.6 %copy-start = (f32[320,128]{1,0:T(8,128)S(1)}, f32[320,128]{1,0:T(8,128)}, u32[]{:S(2)}) copy-start(f32[320,128]{1,0:T(8,128)} %get-tuple-element.9) | copy-start | bytes 491524

commit v5 on v4

--- a/solution.py
+++ b/solution.py
@@ -309,8 +309,8 @@
             copy.start()
         return 0
 
+    lax.fori_loop(1, N_BAND, send_fields, 0)
     lax.fori_loop(1, AHEAD * G, send_records, 0)
-    lax.fori_loop(1, N_BAND, send_fields, 0)
     recv_f[0, 0:ROWS, :] = send_f[pl.ds(pl.multiple_of(tile * ROWS, 8), ROWS), :]
     recv_c[0] = send_c[tile]
     binned[...] = jnp.zeros_like(binned)
@@ -399,6 +399,18 @@
 
     lax.fori_loop(1, N_BAND, sent_fields, 0)
     lax.fori_loop(1, N_TILE, sent_records, 0)
+
+
+def hand_on(conc_in, moved_in, conc_out, moved_out, conc, moved, sem):
+    ins = [pltpu.make_async_copy(moved_in, moved, sem.at[0]), pltpu.make_async_copy(conc_in, conc, sem.at[1])]
+    outs = [pltpu.make_async_copy(moved, moved_out, sem.at[2]), pltpu.make_async_copy(conc, conc_out, sem.at[3])]
+    for copy in ins:
+        copy.start()
+    for before, after in zip(ins, outs):
+        before.wait()
+        after.start()
+    for copy in outs:
+        copy.wait()
 
 
 def shards(wind, temp, diff, removal, frac, height, mass, noise, column, dest):
@@ -426,6 +438,13 @@
             collective_id=0, has_side_effects=True, vmem_limit_bytes=63 * 2**20),
         cost_estimate=pl.CostEstimate(flops=2 * 40960 * 256 * 640, bytes_accessed=2 * 2**20, transcendentals=0),
     )(wind, temp, diff, removal, frac, height, noise, mass, column, dest.reshape(1, B_DEV))
+    conc, moved = pl.pallas_call(
+        hand_on,
+        out_shape=(jax.ShapeDtypeStruct((LEV, COLS), F32), jax.ShapeDtypeStruct((N_TILE * CAP, PB), F32)),
+        in_specs=[hbm] * 2, out_specs=(hbm, hbm),
+        scratch_shapes=[grid, pltpu.VMEM((N_TILE * CAP, PB), F32), dma((4,))],
+        compiler_params=pltpu.CompilerParams(vmem_limit_bytes=63 * 2**20),
+    )(conc, moved)
     return conc[None], moved
 
 

time: 44.1 us -> 43.1 us (0.977)
  local copies, waits for them, and re-layouts: 2.28 us -> 0 us
  Pallas kernels: 41.1 us -> 42.3 us
    unnamed x4 -> x0, local copies, waits for them, and re-layouts: 2.28 us -> none
    pallas_call x0 -> x1, Pallas kernels: none -> 1.67 us  [shards(): pl.pallas_call(hand_on, out_shape=(jax.ShapeDtypeStruct((LEV, COLS), F32)...]
    pallas_call x1, Pallas kernels: 41.1 us -> 40.6 us  [shards(): pl.pallas_call(kernel, out_shape=(jax.ShapeDtypeStruct((LEV, COLS), F32),...]
where the time goes in v5:
time: 43.1 us; the launch traced here: 42.9 us
  Pallas kernels  42.3 us (98%)
  between operations  0.64 us (1%)
    pallas_call x1, Pallas kernels, shards(): pl.pallas_call(kernel, out_shape=(jax.ShapeDtypeStruct((LEV, COLS), F32),...  40.6 us
    pallas_call x1, Pallas kernels, shards(): pl.pallas_call(hand_on, out_shape=(jax.ShapeDtypeStruct((LEV, COLS), F32)...  1.67 us

profile of v5, /device:TPU:1, one launch (start us, length us, event | category | flops | bytes accessed | tf_op | source)
XLA Modules:
  0.0 42.9 jit_solution(3059519556575332370)
XLA Ops:
  0.6 40.6 %shard_map.113 = (f32[128,256]{1,0:T(8,128)}, f32[320,128]{1,0:T(8,128)}) custom-call(bf16[8,16,256]{2,1,0:T(8,128)(2,1)} %wind.1, bf16[8,16,256]{2,1,0:T(8,128)(2,1)} %temp.1, bf16[8,16,256]{2,1,0:T(8,128)(2,1)} %diff.1, bf16[8,16,256]{2,1,0:T(8,128)(2,1)} %removal.1, f32[160,128]{1,0:T(8,128)} %frac.1, f32[160,128]{1,0:T(8,128)} %height.1, ...), custom_call_target="tpu_custom_call" | custom-call | flops 13421772800 | bytes 2097152 | tf_op jit(solution)/shard_map/pallas_call | solution.py:421
  41.2 1.7 %shard_map.114 = (f32[128,256]{1,0:T(8,128)}, f32[320,128]{1,0:T(8,128)}) custom-call(f32[128,256]{1,0:T(8,128)} %get-tuple-element.6.conc_in, f32[320,128]{1,0:T(8,128)} %get-tuple-element.7.moved_in), custom_call_target="tpu_custom_call" | custom-call | tf_op jit(solution)/shard_map/pallas_call | solution.py:441

commit v6 on v5

--- a/solution.py
+++ b/solution.py
@@ -371,9 +371,9 @@
     east = [east_in[:, f * LEV:(f + 1) * LEV] for f in range(4)]
 
     def body(q, carry):
-        lax.fori_loop(q * G, q * G + G, take_records, 0)
         first = jnp.minimum((q + AHEAD - 1) * G, N_TILE)
         lax.fori_loop(first, jnp.minimum(first + G, N_TILE), send_records, 0)
+        lax.fori_loop(q * G, q * G + G, take_records, 0)
         carry, ends = pivots(q, carry[0], upper, lower, inv)
         fr, h, _ = rows_of(q)
         moved, bins = group_work((fr, h, col_of(q)), before_of(q - 1), tperm, val, east)

time: 43.1 us -> 43.2 us (level)
  no operation moved by 1% of the time
where the time goes in v6:
time: 43.2 us; the launch traced here: 42.9 us
  Pallas kernels  42.3 us (98%)
  between operations  0.64 us (1%)
    pallas_call x1, Pallas kernels, shards(): pl.pallas_call(kernel, out_shape=(jax.ShapeDtypeStruct((LEV, COLS), F32),...  40.6 us
    pallas_call x1, Pallas kernels, shards(): pl.pallas_call(hand_on, out_shape=(jax.ShapeDtypeStruct((LEV, COLS), F32)...  1.67 us

profile of v6, /device:TPU:1, one launch (start us, length us, event | category | flops | bytes accessed | tf_op | source)
XLA Modules:
  0.0 42.9 jit_solution(3670038351987625300)
XLA Ops:
  0.6 40.6 %shard_map.113 = (f32[128,256]{1,0:T(8,128)}, f32[320,128]{1,0:T(8,128)}) custom-call(bf16[8,16,256]{2,1,0:T(8,128)(2,1)} %wind.1, bf16[8,16,256]{2,1,0:T(8,128)(2,1)} %temp.1, bf16[8,16,256]{2,1,0:T(8,128)(2,1)} %diff.1, bf16[8,16,256]{2,1,0:T(8,128)(2,1)} %removal.1, f32[160,128]{1,0:T(8,128)} %frac.1, f32[160,128]{1,0:T(8,128)} %height.1, ...), custom_call_target="tpu_custom_call" | custom-call | flops 13421772800 | bytes 2097152 | tf_op jit(solution)/shard_map/pallas_call | solution.py:421
  41.2 1.7 %shard_map.114 = (f32[128,256]{1,0:T(8,128)}, f32[320,128]{1,0:T(8,128)}) custom-call(f32[128,256]{1,0:T(8,128)} %get-tuple-element.6.conc_in, f32[320,128]{1,0:T(8,128)} %get-tuple-element.7.moved_in), custom_call_target="tpu_custom_call" | custom-call | tf_op jit(solution)/shard_map/pallas_call | solution.py:441

commit v7 on v5

--- a/solution.py
+++ b/solution.py
@@ -333,6 +333,16 @@
     east_copy.start()
     split_levels(table, tperm)
     set_kappa(table, upper, lower)
+    def sent_fields(i, _):
+        for f in range(4):
+            field_copy(i, f, (band + i) % N_BAND, band).wait_send()
+        return 0
+
+    def sent_records(i, _):
+        for copy in record_copies(i):
+            copy.wait_send()
+        return 0
+
     def take_records(i, _):
         for copy in record_copies(i):
             copy.wait_recv()
@@ -362,6 +372,7 @@
         for j in range(G):
             moved_ref[pl.ds(place(tile, q * G + j, -1) * CAP, CAP), :] = moved[j * CAP:(j + 1) * CAP]
 
+    lax.fori_loop(1, N_BAND, sent_fields, 0)
     lax.fori_loop(1, G, take_records, 0)
     one = jnp.ones((1, COLS), F32)
     carry = pivots(0, (one, one), upper, lower, inv)
@@ -371,6 +382,7 @@
     east = [east_in[:, f * LEV:(f + 1) * LEV] for f in range(4)]
 
     def body(q, carry):
+        lax.fori_loop(jnp.maximum((q - 1) * G, 1), q * G, sent_records, 0)
         lax.fori_loop(q * G, q * G + G, take_records, 0)
         first = jnp.minimum((q + AHEAD - 1) * G, N_TILE)
         lax.fori_loop(first, jnp.minimum(first + G, N_TILE), send_records, 0)
@@ -387,18 +399,7 @@
     put(NG - 1, moved)
     solve(ends, binned[...] + bins, upper, lower, inv, rhs, fwd, back, conc_ref)
 
-    def sent_fields(i, _):
-        for f in range(4):
-            field_copy(i, f, (band + i) % N_BAND, band).wait_send()
-        return 0
-
-    def sent_records(i, _):
-        for copy in record_copies(i):
-            copy.wait_send()
-        return 0
-
-    lax.fori_loop(1, N_BAND, sent_fields, 0)
-    lax.fori_loop(1, N_TILE, sent_records, 0)
+    lax.fori_loop((NG - 1) * G, N_TILE, sent_records, 0)
 
 
 def hand_on(conc_in, moved_in, conc_out, moved_out, conc, moved, sem):

time: 43.1 us -> 43 us (level)
  no operation moved by 1% of the time
where the time goes in v7:
time: 43 us; the launch traced here: 42.9 us
  Pallas kernels  42.2 us (98%)
  between operations  0.64 us (1%)
    pallas_call x1, Pallas kernels, shards(): pl.pallas_call(kernel, out_shape=(jax.ShapeDtypeStruct((LEV, COLS), F32),...  40.6 us
    pallas_call x1, Pallas kernels, shards(): pl.pallas_call(hand_on, out_shape=(jax.ShapeDtypeStruct((LEV, COLS), F32)...  1.67 us

profile of v7, /device:TPU:1, one launch (start us, length us, event | category | flops | bytes accessed | tf_op | source)
XLA Modules:
  0.0 42.9 jit_solution(5450881473664030124)
XLA Ops:
  0.6 40.6 %shard_map.113 = (f32[128,256]{1,0:T(8,128)}, f32[320,128]{1,0:T(8,128)}) custom-call(bf16[8,16,256]{2,1,0:T(8,128)(2,1)} %wind.1, bf16[8,16,256]{2,1,0:T(8,128)(2,1)} %temp.1, bf16[8,16,256]{2,1,0:T(8,128)(2,1)} %diff.1, bf16[8,16,256]{2,1,0:T(8,128)(2,1)} %removal.1, f32[160,128]{1,0:T(8,128)} %frac.1, f32[160,128]{1,0:T(8,128)} %height.1, ...), custom_call_target="tpu_custom_call" | custom-call | flops 13421772800 | bytes 2097152 | tf_op jit(solution)/shard_map/pallas_call | solution.py:422
  41.2 1.7 %shard_map.114 = (f32[128,256]{1,0:T(8,128)}, f32[320,128]{1,0:T(8,128)}) custom-call(f32[128,256]{1,0:T(8,128)} %get-tuple-element.6.conc_in, f32[320,128]{1,0:T(8,128)} %get-tuple-element.7.moved_in), custom_call_target="tpu_custom_call" | custom-call | tf_op jit(solution)/shard_map/pallas_call | solution.py:442
